TPU v7x, 32 devices: a whole 2x2x4 slice. The times are simulated.
32 devices in a mesh: expert: 4 (over z), mp: 8 (over y, x, core).
Axes of the slice: x: 2, y: 2, z: 4, core: 2. Of those that a mesh axis runs over, the one named last changes fastest.
Arguments:
- x_tokens: bfloat16 [512, 2048], P('expert', 'mp'), may hold values from -6 to 6
- cotangent: bfloat16 [512, 2048], P('expert', 'mp'), may hold values from -2 to 2
- w_gate: bfloat16 [4, 1024, 8192], P('expert', None, 'mp'), may hold values from -0.125 to 0.125
- w_up: bfloat16 [4, 1024, 8192], P('expert', None, 'mp'), may hold values from -0.125 to 0.125
- w_down: bfloat16 [4, 8192, 1024], P('expert', 'mp'), may hold values from -0.125 to 0.125
- combine: float32 [8, 128], P('expert'), may hold values from 0.1 to 1
- indices: int32 [8, 128], replicated, may hold values from -1 to 511, as said below
Outputs:
- grad_tokens: bfloat16 [512, 2048], P('expert', 'mp')
- grad_gate: bfloat16 [4, 1024, 8192], P('expert', None, 'mp')
- grad_up: bfloat16 [4, 1024, 8192], P('expert', None, 'mp')
- grad_down: bfloat16 [4, 8192, 1024], P('expert', 'mp')
- grad_combine: float32 [8, 128], P('expert')
Inputs may be any that keep to these rules, and one draw needn't show every extreme that they name: `indices`: each row lists the tokens one expert chose, in increasing order, then -1 in its remaining slots. Tokens are owned in blocks of 128 along expert; one expert takes at most 64 tokens from one block, and in every row some block gives exactly 64. In every draw some expert fills all 128 slots.
All inputs are finite; a program needn't handle non-finite values.
Results may differ from a plain program's by a relative error of at most 0.022.
Values may be sent and summed in bfloat16 or wider, within the bound.
A program may use at most 64 MiB of HBM per device.

v0:
```python
import functools

import jax
import jax.numpy as jnp
from jax import lax
from jax.experimental import pallas as pl
from jax.experimental.pallas import tpu as pltpu
from jax.sharding import PartitionSpec as P

MESH = pl.DeviceIdType.MESH
F32 = jnp.float32
BF16 = jnp.bfloat16


def nn(a, b):
    return jnp.dot(a, b, preferred_element_type=F32)


def nt(a, b):
    return lax.dot_general(a, b, (((1,), (1,)), ((), ())), preferred_element_type=F32)


def tn(a, b):
    return lax.dot_general(a, b, (((0,), (0,)), ((), ())), preferred_element_type=F32)


def layer_kernel(
    dims,
    x_hbm, cot_hbm, wg_hbm, wu_hbm, wd_hbm, combine_hbm, idx_hbm,
    tokens_ref, terms_ref, grad_gate, grad_up, grad_down,
    rows_in_ref, scaled_ref, act_ref, dgate_ref, dup_ref,
    x_ref, combine_ref, idx_ref, wg, wu, wd, tok, gathered, rx, rows_out, mine, ex_send, ex_recv,
    term_buf, red_send, red_recv, xs_send, xs_recv, bk_send, bk_recv, place,
    w_sem, z_send, z_recv, m_send, m_recv, f_send, x_send, x_recv,
    c_send, c_recv, r_send, r_recv, s_send, s_recv, sf_send, k_send, k_recv,
):
    (groups, lanes, exp_dev, blocks, half_lanes, tok_dev, width, capacity, hidden, chunk, peer) = dims
    half_width = half_lanes * width
    experts = groups * exp_dev
    chunks = hidden // chunk
    z = lax.axis_index("expert")
    lane = lax.axis_index("mp")
    own_b = lax.rem(lane, blocks)
    own_h = lax.rem(lax.div(lane, blocks), 2)
    own_e = lax.div(lane, 2 * blocks)
    feat_half = lax.div(lane, half_lanes)
    feat_pos = lax.rem(lane, half_lanes)

    def lane_of(e, h, b):
        return (e * 2 + h) * blocks + b

    def remote(src, dst, ssem, rsem, to_z, to_lane):
        return pltpu.make_async_remote_copy(
            src_ref=src, dst_ref=dst, send_sem=ssem, recv_sem=rsem,
            device_id=(to_z, to_lane), device_id_type=MESH,
        )

    def arrived(ref, ssem, rsem):
        remote(ref, ref, ssem, rsem, z, lane).wait_recv()

    loads = [
        pltpu.make_async_copy(src, dst, w_sem.at[i])
        for i, (src, dst) in enumerate((
            (idx_hbm, idx_ref), (x_hbm, x_ref), (combine_hbm, combine_ref), (cot_hbm, tok.at[z]),
            (wg_hbm.at[0], wg), (wu_hbm.at[0], wu), (wd_hbm.at[0], wd),
        ))
    ]
    for load in loads:
        load.start()

    barrier = pltpu.get_barrier_semaphore()
    for d in range(1, groups):
        pl.semaphore_signal(barrier, inc=1, device_id=(lax.rem(z + d, groups), lane), device_id_type=MESH)
        for e in range(exp_dev):
            for other in (lane_of(e, feat_half, own_b), own_h * half_lanes + e * blocks + own_b):
                pl.semaphore_signal(barrier, inc=1, device_id=(lax.rem(z + d, groups), other), device_id_type=MESH)
    for d in range(1, lanes):
        pl.semaphore_signal(barrier, inc=1, device_id=(z, lax.rem(lane + d, lanes)), device_id_type=MESH)
    def iota(shape, axis):
        return lax.broadcasted_iota(jnp.int32, shape, axis)

    def before(row, g):
        return jnp.sum(jnp.where((row >= 0) & (row < g * tok_dev), 1.0, 0.0), axis=1, keepdims=True)

    def ones_where(condition):
        return jnp.where(condition, 1.0, 0.0).astype(BF16)

    def token_slot(row):
        return ones_where(iota((tok_dev, capacity), 0) + z * tok_dev == row)

    def row_slot(row, g):
        ahead = iota((peer, capacity), 1) - iota((peer, capacity), 0)
        return ones_where(ahead.astype(F32) == before(row, g))

    loads[0].wait()
    loads[1].wait()
    for d in range(groups):
        g = lax.rem(z + d, groups)
        for e in range(exp_dev):
            row = idx_ref[pl.ds(g * exp_dev + e, 1), :]
            pick = nt(row_slot(row, z), token_slot(row)).astype(BF16)
            xs_send[d, e] = nn(pick, x_ref[...]).astype(BF16)

    pl.semaphore_wait(barrier, lanes - 1 + (groups - 1) * (1 + 2 * exp_dev))

    sends = []

    def send_rows(d, e):
        return remote(xs_send.at[d, e], xs_recv.at[feat_pos, z], s_send.at[d, e], s_recv.at[feat_pos, z],
                      lax.rem(z + d, groups), lane_of(e, feat_half, own_b))

    for d in range(1, groups):
        for e in range(exp_dev):
            copy = send_rows(d, e)
            copy.start()
            sends.append(copy)
    for e in range(exp_dev):
        target = lane_of(e, feat_half, own_b)

        @pl.when(target == lane)
        def _():
            xs_recv[feat_pos, z] = xs_send[0, e]

        @pl.when(target != lane)
        def _():
            send_rows(0, e).start()

    eye = iota((capacity, capacity), 0) == iota((capacity, capacity), 1)

    def column(row):
        return jnp.sum(jnp.where(eye, jnp.broadcast_to(row, (capacity, capacity)), 0.0), axis=1, keepdims=True)

    idx_rows = [idx_ref[pl.ds(z * exp_dev + e, 1), :] for e in range(exp_dev)]
    idx_cols = [column(row.astype(F32)).astype(jnp.int32) for row in idx_rows]
    loads[2].wait()
    weight = column(combine_ref[pl.ds(own_e, 1), :])
    own_row = idx_ref[pl.ds(z * exp_dev + own_e, 1), :]

    def slot_map(axis):
        shape = (capacity, groups * peer) if axis else (groups * peer, capacity)
        spot, slot = iota(shape, axis), iota(shape, 1 - axis)
        total = jnp.zeros(shape, F32)
        for g in range(groups):
            hit = (slot - spot + g * peer).astype(F32) == before(own_row, g)
            total += jnp.where(hit & (spot >= g * peer) & (spot < (g + 1) * peer), 1.0, 0.0)
        return total.astype(BF16)

    to_slots = slot_map(1)
    for d in range(groups):
        zs = lax.rem(z + d, groups)
        for j in range(exp_dev):
            p = j * blocks + own_b
            source = own_h * half_lanes + p

            @pl.when((source != lane) | (d > 0))
            def _():
                arrived(xs_recv.at[p, zs], s_send.at[0, 0], s_recv.at[p, zs])

            for n in range(1, blocks):
                copy = remote(xs_recv.at[p, zs], xs_recv.at[p, zs], sf_send.at[j, zs, n], s_recv.at[p, zs],
                              z, lane_of(own_e, own_h, lax.rem(own_b + n, blocks)))
                copy.start()
                sends.append(copy)

    loads[3].wait()
    for d in range(1, groups):
        copy = remote(tok.at[z], tok.at[z], z_send.at[d], z_recv.at[z], lax.rem(z + d, groups), lane)
        copy.start()
        sends.append(copy)

    for d in range(groups):
        zs = lax.rem(z + d, groups)
        for n in range(1, blocks):
            for j in range(exp_dev):
                p = j * blocks + lax.rem(own_b + n, blocks)
                arrived(xs_recv.at[p, zs], s_send.at[0, 0], s_recv.at[p, zs])
    for p in range(half_lanes):
        packed = xs_recv[p].reshape(groups * peer, width)
        rows_in_ref[:, p * width:(p + 1) * width] = nn(to_slots, packed).astype(BF16)

    def exchange_rows():
        for d in range(1, groups):
            s = lax.rem(z + d, groups)
            arrived(tok.at[s], z_send.at[d], z_recv.at[s])
        for e in range(exp_dev):
            total = jnp.zeros((capacity, width), F32)
            for g in range(groups):
                ids = iota((capacity, tok_dev), 1) + g * tok_dev
                pick = ones_where(ids == idx_cols[e])
                total += nn(pick, tok[g])
            gathered[e] = total.astype(BF16)
            target = lane_of(e, feat_half, own_b)

            @pl.when(target == lane)
            def _():
                rx[feat_pos] = gathered[e]

            @pl.when(target != lane)
            def _():
                remote(gathered.at[e], rx.at[feat_pos], m_send.at[e],
                       m_recv.at[feat_pos], z, target).start()

        for j in range(exp_dev):
            p = j * blocks + own_b
            source = own_h * half_lanes + p

            @pl.when(source != lane)
            def _():
                arrived(rx.at[p], m_send.at[0], m_recv.at[p])

            for d in range(1, blocks):
                copy = remote(rx.at[p], rx.at[p], f_send.at[j, d], m_recv.at[p],
                              z, lane_of(own_e, own_h, lax.rem(own_b + d, blocks)))
                copy.start()
                sends.append(copy)
        for d in range(1, blocks):
            for j in range(exp_dev):
                p = j * blocks + lax.rem(own_b + d, blocks)
                arrived(rx.at[p], m_send.at[0], m_recv.at[p])

    partner = lane_of(own_e, 1 - own_h, own_b)

    def exchange_sum(which, c, value):
        cols = slice(c * chunk, (c + 1) * chunk)
        mine[which, :, cols] = value
        ex_send[which, c] = value.astype(BF16)
        copy = remote(ex_send.at[which, c], ex_recv.at[which, c], x_send.at[which, c],
                      x_recv.at[which, c], z, partner)
        copy.start()
        sends.append(copy)

    loads[4].wait()
    loads[5].wait()
    for c in range(chunks):
        cols = slice(c * chunk, (c + 1) * chunk)
        exchange_sum(0, c, nn(rows_in_ref[...], wg[:, cols]))
        exchange_sum(1, c, nn(rows_in_ref[...], wu[:, cols]))

    exchange_rows()
    for p in range(half_lanes):
        part = rx[p]
        rows_out[:, p * width:(p + 1) * width] = part
        scaled_ref[:, p * width:(p + 1) * width] = (weight * part.astype(F32)).astype(BF16)
    loads[6].wait()
    for c in range(chunks):
        cols = slice(c * chunk, (c + 1) * chunk)
        exchange_sum(2, c, nt(rows_out[...], wd[cols, :]))

    slot_term = jnp.zeros((capacity, 1), F32)
    for c in range(chunks):
        cols = slice(c * chunk, (c + 1) * chunk)
        for which in range(3):
            arrived(ex_recv.at[which, c], x_send.at[which, c], x_recv.at[which, c])
        gate = mine[0, :, cols] + ex_recv[0, c].astype(F32)
        up = mine[1, :, cols] + ex_recv[1, c].astype(F32)
        back = mine[2, :, cols] + ex_recv[2, c].astype(F32)
        s = jax.nn.sigmoid(gate)
        act = (gate * s * up).astype(BF16)
        act_ref[:, cols] = act
        slot_term += jnp.sum(act.astype(F32) * back, axis=1, keepdims=True)
        a = weight * back
        dgate_ref[:, cols] = (a * up * s * (1.0 + gate * (1.0 - s))).astype(BF16)
        dup_ref[:, cols] = (a * gate * s).astype(BF16)

    def block_part(p):
        rows = pl.ds(pl.multiple_of(p * width, width), width)
        return nt(dgate_ref[...], wg[rows, :]) + nt(dup_ref[...], wu[rows, :])

    for d in range(1, blocks):
        to_b = lax.rem(own_b + d, blocks)
        for j in range(exp_dev):
            red_send[d, j] = block_part(j * blocks + to_b).astype(BF16)
            copy = remote(red_send.at[d, j], red_recv.at[own_b, j], r_send.at[d, j], r_recv.at[own_b, j],
                          z, lane_of(own_e, own_h, to_b))
            copy.start()
            sends.append(copy)
    from_slots = slot_map(0)

    def send_back(j, d):
        g = lax.rem(z + d, groups)
        slot = z * exp_dev + own_e
        return remote(bk_send.at[j, g], bk_recv.at[slot], k_send.at[j, d], k_recv.at[slot],
                      g, own_h * half_lanes + j * blocks + own_b)

    for j in range(exp_dev):
        total = block_part(j * blocks + own_b).astype(BF16).astype(F32)
        for d in range(1, blocks):
            from_b = lax.rem(own_b + d, blocks)
            arrived(red_recv.at[from_b, j], r_send.at[d, j], r_recv.at[from_b, j])
            total += red_recv[from_b, j].astype(F32)
        bk_send[j] = nn(from_slots, total.astype(BF16)).astype(BF16).reshape(groups, peer, width)
        for d in range(1, groups):
            copy = send_back(j, d)
            copy.start()
            sends.append(copy)
        target = own_h * half_lanes + j * blocks + own_b

        @pl.when(target == lane)
        def _():
            bk_recv[z * exp_dev + own_e] = bk_send[j, z]

        @pl.when(target != lane)
        def _():
            send_back(j, 0).start()

    term_row = jnp.sum(jnp.where(eye, jnp.broadcast_to(slot_term, (capacity, capacity)), 0.0), axis=0, keepdims=True)

    @pl.when(own_h == 0)
    def _():
        term_buf[own_e, own_b] = jnp.broadcast_to(term_row, (8, capacity))
        for d in range(1, lanes):
            remote(term_buf.at[own_e, own_b], term_buf.at[own_e, own_b], c_send.at[d],
                   c_recv.at[own_e, own_b], z, lax.rem(lane + d, lanes)).start()

    step = min(half_width, 256)
    for i in range(half_width // step):
        cols = slice(i * step, (i + 1) * step)
        grad_gate[0, cols, :] = tn(rows_in_ref[:, cols], dgate_ref[...]).astype(BF16)
        grad_up[0, cols, :] = tn(rows_in_ref[:, cols], dup_ref[...]).astype(BF16)
    for c in range(chunks):
        cols = slice(c * chunk, (c + 1) * chunk)
        grad_down[0, cols, :] = tn(act_ref[:, cols], scaled_ref[...]).astype(BF16)
    for e in range(experts):
        row = idx_ref[e:e + 1, :]
        place[e] = nt(token_slot(row), row_slot(row, z)).astype(BF16)

    for e in range(exp_dev):
        for b in range(blocks):
            @pl.when(lane_of(e, 0, b) != lane)
            def _():
                arrived(term_buf.at[e, b], c_send.at[1], c_recv.at[e, b])
        row = term_buf[e, 0, 0:1, :]
        for b in range(1, blocks):
            row += term_buf[e, b, 0:1, :]
        terms_ref[e:e + 1, :] = row

    total = jnp.zeros((tok_dev, width), F32)
    for d in range(groups):
        zs = lax.rem(z + d, groups)
        for e in range(exp_dev):
            slot = zs * exp_dev + e

            @pl.when((lane_of(e, feat_half, own_b) != lane) | (d > 0))
            def _():
                arrived(bk_recv.at[slot], k_send.at[0, 0], k_recv.at[slot])

            total += nn(place[slot], bk_recv[slot])
    tokens_ref[...] = total.astype(BF16)

    for copy in sends:
        copy.wait_send()
    for e in range(exp_dev):
        target = lane_of(e, feat_half, own_b)

        @pl.when(target != lane)
        def _():
            send_rows(0, e).wait_send()
            remote(gathered.at[e], rx.at[feat_pos], m_send.at[e], m_recv.at[feat_pos], z, target).wait_send()

    for j in range(exp_dev):
        @pl.when(own_h * half_lanes + j * blocks + own_b != lane)
        def _():
            send_back(j, 0).wait_send()

    @pl.when(own_h == 0)
    def _():
        for d in range(1, lanes):
            remote(term_buf.at[own_e, own_b], term_buf.at[own_e, own_b], c_send.at[d],
                   c_recv.at[own_e, own_b], z, lax.rem(lane + d, lanes)).wait_send()


def write_kernel(*refs):
    count = len(refs) // 2
    copies = [
        pltpu.make_async_copy(src, dst, refs[-1].at[i])
        for i, (src, dst) in enumerate(zip(refs[:count], refs[count:2 * count]))
    ]
    for copy in copies:
        copy.start()
    for copy in copies:
        copy.wait()


def local(x_tokens, cotangent, w_gate, w_up, w_down, combine, indices):
    groups = lax.axis_size("expert")
    lanes = lax.axis_size("mp")
    tok_dev, width = x_tokens.shape
    experts, capacity = indices.shape
    exp_dev = experts // groups
    blocks = lanes // (2 * exp_dev)
    half_lanes = lanes // 2
    half_width, hidden = w_gate.shape[1:]
    chunk = min(hidden, 256)
    chunks = hidden // chunk
    peer = max(2 * capacity // groups, 16)
    dims = (groups, lanes, exp_dev, blocks, half_lanes, tok_dev, width, capacity, hidden, chunk, peer)
    vmem = pl.BlockSpec(memory_space=pltpu.VMEM)
    anywhere = pl.BlockSpec(memory_space=pl.ANY)
    dma = pltpu.SemaphoreType.DMA
    slot_half = jax.ShapeDtypeStruct((capacity, half_width), BF16)
    slot_hidden = jax.ShapeDtypeStruct((capacity, hidden), BF16)
    results = [
        jax.ShapeDtypeStruct((tok_dev, width), BF16),
        jax.ShapeDtypeStruct((exp_dev, capacity), F32),
        jax.ShapeDtypeStruct(w_gate.shape, BF16),
        jax.ShapeDtypeStruct(w_up.shape, BF16),
        jax.ShapeDtypeStruct(w_down.shape, BF16),
    ]
    operands = [
        pltpu.with_memory_space_constraint(a, pltpu.HBM)
        for a in (x_tokens, cotangent, w_gate, w_up, w_down, combine, indices)
    ]
    held = pl.pallas_call(
        functools.partial(layer_kernel, dims),
        out_shape=results,
        in_specs=[pl.BlockSpec(memory_space=pltpu.HBM)] * 7,
        out_specs=[vmem] * 5,
        scratch_shapes=[
            pltpu.VMEM((capacity, half_width), BF16),
            pltpu.VMEM((capacity, half_width), BF16),
            pltpu.VMEM((capacity, hidden), BF16),
            pltpu.VMEM((capacity, hidden), BF16),
            pltpu.VMEM((capacity, hidden), BF16),
            pltpu.VMEM((tok_dev, width), BF16),
            pltpu.VMEM((exp_dev, capacity), F32),
            pltpu.VMEM((experts, capacity), jnp.int32),
            pltpu.VMEM((half_width, hidden), BF16),
            pltpu.VMEM((half_width, hidden), BF16),
            pltpu.VMEM((hidden, half_width), BF16),
            pltpu.VMEM((groups, tok_dev, width), BF16),
            pltpu.VMEM((exp_dev, capacity, width), BF16),
            pltpu.VMEM((half_lanes, capacity, width), BF16),
            pltpu.VMEM((capacity, half_width), BF16),
            pltpu.VMEM((3, capacity, hidden), F32),
            pltpu.VMEM((3, chunks, capacity, chunk), BF16),
            pltpu.VMEM((3, chunks, capacity, chunk), BF16),
            pltpu.VMEM((exp_dev, blocks, 8, capacity), F32),
            pltpu.VMEM((blocks, exp_dev, capacity, width), BF16),
            pltpu.VMEM((blocks, exp_dev, capacity, width), BF16),
            pltpu.VMEM((groups, exp_dev, peer, width), BF16),
            pltpu.VMEM((half_lanes, groups, peer, width), BF16),
            pltpu.VMEM((exp_dev, groups, peer, width), BF16),
            pltpu.VMEM((experts, peer, width), BF16),
            pltpu.VMEM((experts, tok_dev, peer), BF16),
            dma((7,)), dma((groups,)), dma((groups,)),
            dma((exp_dev,)), dma((half_lanes,)), dma((exp_dev, blocks)),
            dma((3, chunks)), dma((3, chunks)),
            dma((lanes,)), dma((exp_dev, blocks)),
            dma((blocks, exp_dev)), dma((blocks, exp_dev)),
            dma((groups, exp_dev)), dma((half_lanes, groups)), dma((exp_dev, groups, blocks)),
            dma((exp_dev, groups)), dma((experts,)),
        ],
        compiler_params=pltpu.CompilerParams(
            collective_id=0, has_side_effects=True, vmem_limit_bytes=40 * 1024 * 1024
        ),
        name="layer",
    )(*operands)
    grad_tokens, grad_combine, grad_gate, grad_up, grad_down = pl.pallas_call(
        write_kernel,
        out_shape=results,
        in_specs=[anywhere] * 5,
        out_specs=[anywhere] * 5,
        scratch_shapes=[dma((5,))],
        compiler_params=pltpu.CompilerParams(vmem_limit_bytes=1024 * 1024),
        name="write_out",
    )(*[pltpu.with_memory_space_constraint(a, pltpu.VMEM) for a in held])
    return grad_tokens, grad_gate, grad_up, grad_down, grad_combine


def solution(mesh):
    placed = (
        P("expert", "mp"),
        P("expert", "mp"),
        P("expert", None, "mp"),
        P("expert", None, "mp"),
        P("expert", "mp", None),
        P("expert", None),
        P(),
    )
    return jax.shard_map(
        local,
        mesh=mesh,
        in_specs=placed,
        out_specs=(
            P("expert", "mp"),
            P("expert", None, "mp"),
            P("expert", None, "mp"),
            P("expert", "mp", None),
            P("expert", None),
        ),
        check_vma=False,
    )
```

profile of v0, /device:TPU:2, one launch (start us, length us, event | category | flops | bytes accessed | tf_op | source)
XLA Modules:
  0.0 53.1 jit_solution(2826270279592586819)
XLA Ops:
  0.6 49.7 %layer.1 = (bf16[128,256]{1,0:T(8,128)(2,1)S(1)}, f32[2,128]{1,0:T(2,128)S(1)}, bf16[1,1024,1024]{2,1,0:T(8,128)(2,1)S(1)}, bf16[1,1024,1024]{2,1,0:T(8,128)(2,1)S(1)}, bf16[1,1024,1024]{2,1,0:T(8,128)(2,1)S(1)}) custom-call(bf16[128,256]{1,0:T(8,128)(2,1)} %x_hbm.1, bf16[128,256]{1,0:T(8,128)(2,1)} %cot_hbm.1, bf16[1,1024,1024]{2,1,0:T(8,128)(2,1)} %wg_hbm.1, ...), custom_call_target="tpu_custom_call" | custom-call | tf_op jit(solution)/shard_map/layer/pallas_call | solution.py:413
  50.3 2.8 %write_out.1 = (bf16[128,256]{1,0:T(8,128)(2,1)}, f32[2,128]{1,0:T(2,128)}, bf16[1,1024,1024]{2,1,0:T(8,128)(2,1)}, bf16[1,1024,1024]{2,1,0:T(8,128)(2,1)}, bf16[1,1024,1024]{2,1,0:T(8,128)(2,1)}) custom-call(bf16[128,256]{1,0:T(8,128)(2,1)S(1)} %get-tuple-element.15.refs_0_, f32[2,128]{1,0:T(2,128)S(1)} %get-tuple-element.16.refs_1_, ...), custom_call_target="tpu_custom_call" | custom-call | tf_op jit(solution)/shard_map/write_out/pallas_call | solution.py:458
where the time goes:
time: 53.3 us; the launch traced here: 53.1 us
  Pallas kernels  52.5 us (98%)
  between operations  0.64 us (1%)
    pallas_call x1, Pallas kernels, local(): pl.pallas_call(functools.partial(layer_kernel, dims), out_shape=results,...  49.7 us
    pallas_call x1, Pallas kernels, local(): pl.pallas_call(write_kernel, out_shape=results, in_specs=[anywhere] * 5,...  2.77 us

commit v1 on v0

--- a/solution.py
+++ b/solution.py
@@ -29,9 +29,9 @@
     x_hbm, cot_hbm, wg_hbm, wu_hbm, wd_hbm, combine_hbm, idx_hbm,
     tokens_ref, terms_ref, grad_gate, grad_up, grad_down,
     rows_in_ref, scaled_ref, act_ref, dgate_ref, dup_ref,
-    x_ref, combine_ref, idx_ref, wg, wu, wd, tok, gathered, rx, rows_out, mine, ex_send, ex_recv,
-    term_buf, red_send, red_recv, xs_send, xs_recv, bk_send, bk_recv, place,
-    w_sem, z_send, z_recv, m_send, m_recv, f_send, x_send, x_recv,
+    x_ref, cot_ref, combine_ref, idx_ref, wg, wu, wd, rows_out, mine, ex_send, ex_recv,
+    term_buf, red_send, red_recv, xs_send, xs_recv, bk_send, bk_recv, place, acc,
+    w_sem, x_send, x_recv,
     c_send, c_recv, r_send, r_recv, s_send, s_recv, sf_send, k_send, k_recv,
 ):
     (groups, lanes, exp_dev, blocks, half_lanes, tok_dev, width, capacity, hidden, chunk, peer) = dims
@@ -61,7 +61,7 @@
     loads = [
         pltpu.make_async_copy(src, dst, w_sem.at[i])
         for i, (src, dst) in enumerate((
-            (idx_hbm, idx_ref), (x_hbm, x_ref), (combine_hbm, combine_ref), (cot_hbm, tok.at[z]),
+            (idx_hbm, idx_ref), (x_hbm, x_ref), (combine_hbm, combine_ref), (cot_hbm, cot_ref),
             (wg_hbm.at[0], wg), (wu_hbm.at[0], wu), (wd_hbm.at[0], wd),
         ))
     ]
@@ -94,44 +94,54 @@
 
     loads[0].wait()
     loads[1].wait()
+    loads[3].wait()
     for d in range(groups):
         g = lax.rem(z + d, groups)
         for e in range(exp_dev):
             row = idx_ref[pl.ds(g * exp_dev + e, 1), :]
             pick = nt(row_slot(row, z), token_slot(row)).astype(BF16)
-            xs_send[d, e] = nn(pick, x_ref[...]).astype(BF16)
+            xs_send[0, d, e] = nn(pick, x_ref[...]).astype(BF16)
+            xs_send[1, d, e] = nn(pick, cot_ref[...]).astype(BF16)
 
     pl.semaphore_wait(barrier, lanes - 1 + (groups - 1) * (1 + 2 * exp_dev))
 
     sends = []
 
-    def send_rows(d, e):
-        return remote(xs_send.at[d, e], xs_recv.at[feat_pos, z], s_send.at[d, e], s_recv.at[feat_pos, z],
-                      lax.rem(z + d, groups), lane_of(e, feat_half, own_b))
-
-    for d in range(1, groups):
+    def send_rows(kind, d, e):
+        return remote(xs_send.at[kind, d, e], xs_recv.at[kind, feat_pos, z], s_send.at[kind, d, e],
+                      s_recv.at[kind, feat_pos, z], lax.rem(z + d, groups), lane_of(e, feat_half, own_b))
+
+    def start_rows(kind):
+        for d in range(1, groups):
+            for e in range(exp_dev):
+                send_rows(kind, d, e).start()
         for e in range(exp_dev):
-            copy = send_rows(d, e)
-            copy.start()
-            sends.append(copy)
-    for e in range(exp_dev):
-        target = lane_of(e, feat_half, own_b)
-
-        @pl.when(target == lane)
-        def _():
-            xs_recv[feat_pos, z] = xs_send[0, e]
-
-        @pl.when(target != lane)
-        def _():
-            send_rows(0, e).start()
+            target = lane_of(e, feat_half, own_b)
+
+            @pl.when(target == lane)
+            def _():
+                xs_recv[kind, feat_pos, z] = xs_send[kind, 0, e]
+
+            @pl.when(target != lane)
+            def _():
+                send_rows(kind, 0, e).start()
+
+    def finish_rows(kind):
+        for d in range(1, groups):
+            for e in range(exp_dev):
+                send_rows(kind, d, e).wait_send()
+        for e in range(exp_dev):
+            @pl.when(lane_of(e, feat_half, own_b) != lane)
+            def _():
+                send_rows(kind, 0, e).wait_send()
+
+    start_rows(0)
 
     eye = iota((capacity, capacity), 0) == iota((capacity, capacity), 1)
 
     def column(row):
         return jnp.sum(jnp.where(eye, jnp.broadcast_to(row, (capacity, capacity)), 0.0), axis=1, keepdims=True)
 
-    idx_rows = [idx_ref[pl.ds(z * exp_dev + e, 1), :] for e in range(exp_dev)]
-    idx_cols = [column(row.astype(F32)).astype(jnp.int32) for row in idx_rows]
     loads[2].wait()
     weight = column(combine_ref[pl.ds(own_e, 1), :])
     own_row = idx_ref[pl.ds(z * exp_dev + own_e, 1), :]
@@ -146,77 +156,36 @@
         return total.astype(BF16)
 
     to_slots = slot_map(1)
-    for d in range(groups):
-        zs = lax.rem(z + d, groups)
-        for j in range(exp_dev):
-            p = j * blocks + own_b
-            source = own_h * half_lanes + p
-
-            @pl.when((source != lane) | (d > 0))
-            def _():
-                arrived(xs_recv.at[p, zs], s_send.at[0, 0], s_recv.at[p, zs])
-
+
+    def arrive_rows(kind, rows_ref):
+        for d in range(groups):
+            zs = lax.rem(z + d, groups)
+            for j in range(exp_dev):
+                p = j * blocks + own_b
+                source = own_h * half_lanes + p
+
+                @pl.when((source != lane) | (d > 0))
+                def _():
+                    arrived(xs_recv.at[kind, p, zs], s_send.at[kind, 0, 0], s_recv.at[kind, p, zs])
+
+                for n in range(1, blocks):
+                    copy = remote(xs_recv.at[kind, p, zs], xs_recv.at[kind, p, zs], sf_send.at[kind, j, zs, n],
+                                  s_recv.at[kind, p, zs], z, lane_of(own_e, own_h, lax.rem(own_b + n, blocks)))
+                    copy.start()
+                    sends.append(copy)
+        for d in range(groups):
+            zs = lax.rem(z + d, groups)
             for n in range(1, blocks):
-                copy = remote(xs_recv.at[p, zs], xs_recv.at[p, zs], sf_send.at[j, zs, n], s_recv.at[p, zs],
-                              z, lane_of(own_e, own_h, lax.rem(own_b + n, blocks)))
-                copy.start()
-                sends.append(copy)
-
-    loads[3].wait()
-    for d in range(1, groups):
-        copy = remote(tok.at[z], tok.at[z], z_send.at[d], z_recv.at[z], lax.rem(z + d, groups), lane)
-        copy.start()
-        sends.append(copy)
-
-    for d in range(groups):
-        zs = lax.rem(z + d, groups)
-        for n in range(1, blocks):
-            for j in range(exp_dev):
-                p = j * blocks + lax.rem(own_b + n, blocks)
-                arrived(xs_recv.at[p, zs], s_send.at[0, 0], s_recv.at[p, zs])
-    for p in range(half_lanes):
-        packed = xs_recv[p].reshape(groups * peer, width)
-        rows_in_ref[:, p * width:(p + 1) * width] = nn(to_slots, packed).astype(BF16)
-
-    def exchange_rows():
-        for d in range(1, groups):
-            s = lax.rem(z + d, groups)
-            arrived(tok.at[s], z_send.at[d], z_recv.at[s])
-        for e in range(exp_dev):
-            total = jnp.zeros((capacity, width), F32)
-            for g in range(groups):
-                ids = iota((capacity, tok_dev), 1) + g * tok_dev
-                pick = ones_where(ids == idx_cols[e])
-                total += nn(pick, tok[g])
-            gathered[e] = total.astype(BF16)
-            target = lane_of(e, feat_half, own_b)
-
-            @pl.when(target == lane)
-            def _():
-                rx[feat_pos] = gathered[e]
-
-            @pl.when(target != lane)
-            def _():
-                remote(gathered.at[e], rx.at[feat_pos], m_send.at[e],
-                       m_recv.at[feat_pos], z, target).start()
-
-        for j in range(exp_dev):
-            p = j * blocks + own_b
-            source = own_h * half_lanes + p
-
-            @pl.when(source != lane)
-            def _():
-                arrived(rx.at[p], m_send.at[0], m_recv.at[p])
-
-            for d in range(1, blocks):
-                copy = remote(rx.at[p], rx.at[p], f_send.at[j, d], m_recv.at[p],
-                              z, lane_of(own_e, own_h, lax.rem(own_b + d, blocks)))
-                copy.start()
-                sends.append(copy)
-        for d in range(1, blocks):
-            for j in range(exp_dev):
-                p = j * blocks + lax.rem(own_b + d, blocks)
-                arrived(rx.at[p], m_send.at[0], m_recv.at[p])
+                for j in range(exp_dev):
+                    p = j * blocks + lax.rem(own_b + n, blocks)
+                    arrived(xs_recv.at[kind, p, zs], s_send.at[kind, 0, 0], s_recv.at[kind, p, zs])
+        for p in range(half_lanes):
+            packed = xs_recv[kind, p].reshape(groups * peer, width)
+            rows_ref[:, p * width:(p + 1) * width] = nn(to_slots, packed).astype(BF16)
+
+    finish_rows(0)
+    start_rows(1)
+    arrive_rows(0, rows_in_ref)
 
     partner = lane_of(own_e, 1 - own_h, own_b)
 
@@ -236,35 +205,50 @@
         exchange_sum(0, c, nn(rows_in_ref[...], wg[:, cols]))
         exchange_sum(1, c, nn(rows_in_ref[...], wu[:, cols]))
 
-    exchange_rows()
-    for p in range(half_lanes):
-        part = rx[p]
-        rows_out[:, p * width:(p + 1) * width] = part
-        scaled_ref[:, p * width:(p + 1) * width] = (weight * part.astype(F32)).astype(BF16)
+    arrive_rows(1, rows_out)
+    scaled_ref[...] = (weight * rows_out[...].astype(F32)).astype(BF16)
     loads[6].wait()
     for c in range(chunks):
         cols = slice(c * chunk, (c + 1) * chunk)
         exchange_sum(2, c, nt(rows_out[...], wd[cols, :]))
 
+    def sum_arrived(which, c):
+        arrived(ex_recv.at[which, c], x_send.at[which, c], x_recv.at[which, c])
+        return mine[which, :, c * chunk:(c + 1) * chunk] + ex_recv[which, c].astype(F32)
+
+    for c in range(chunks):
+        cols = slice(c * chunk, (c + 1) * chunk)
+        gate = sum_arrived(0, c)
+        up = sum_arrived(1, c)
+        s = jax.nn.sigmoid(gate)
+        swish = gate * s
+        act_ref[:, cols] = (swish * up).astype(BF16)
+        mine[0, :, cols] = up * s * (1.0 + gate * (1.0 - s))
+        mine[1, :, cols] = swish
+        grad_down[0, cols, :] = tn(act_ref[:, cols], scaled_ref[...]).astype(BF16)
+
+    def part_of(p, cols):
+        rows = pl.ds(pl.multiple_of(p * width, width), width)
+        return nt(dgate_ref[:, cols], wg[rows, cols]) + nt(dup_ref[:, cols], wu[rows, cols])
+
     slot_term = jnp.zeros((capacity, 1), F32)
     for c in range(chunks):
         cols = slice(c * chunk, (c + 1) * chunk)
-        for which in range(3):
-            arrived(ex_recv.at[which, c], x_send.at[which, c], x_recv.at[which, c])
-        gate = mine[0, :, cols] + ex_recv[0, c].astype(F32)
-        up = mine[1, :, cols] + ex_recv[1, c].astype(F32)
-        back = mine[2, :, cols] + ex_recv[2, c].astype(F32)
-        s = jax.nn.sigmoid(gate)
-        act = (gate * s * up).astype(BF16)
-        act_ref[:, cols] = act
-        slot_term += jnp.sum(act.astype(F32) * back, axis=1, keepdims=True)
+        back = sum_arrived(2, c)
+        slot_term += jnp.sum(act_ref[:, cols].astype(F32) * back, axis=1, keepdims=True)
         a = weight * back
-        dgate_ref[:, cols] = (a * up * s * (1.0 + gate * (1.0 - s))).astype(BF16)
-        dup_ref[:, cols] = (a * gate * s).astype(BF16)
+        dgate_ref[:, cols] = (a * mine[0, :, cols]).astype(BF16)
+        dup_ref[:, cols] = (a * mine[1, :, cols]).astype(BF16)
+        if c < chunks - 1:
+            for p in range(half_lanes):
+                if c == 0:
+                    acc[p] = part_of(p, cols)
+                else:
+                    acc[p] += part_of(p, cols)
 
     def block_part(p):
-        rows = pl.ds(pl.multiple_of(p * width, width), width)
-        return nt(dgate_ref[...], wg[rows, :]) + nt(dup_ref[...], wu[rows, :])
+        last = part_of(p, slice((chunks - 1) * chunk, hidden))
+        return acc[p] + last if chunks > 1 else last
 
     for d in range(1, blocks):
         to_b = lax.rem(own_b + d, blocks)
@@ -317,9 +301,6 @@
         cols = slice(i * step, (i + 1) * step)
         grad_gate[0, cols, :] = tn(rows_in_ref[:, cols], dgate_ref[...]).astype(BF16)
         grad_up[0, cols, :] = tn(rows_in_ref[:, cols], dup_ref[...]).astype(BF16)
-    for c in range(chunks):
-        cols = slice(c * chunk, (c + 1) * chunk)
-        grad_down[0, cols, :] = tn(act_ref[:, cols], scaled_ref[...]).astype(BF16)
     for e in range(experts):
         row = idx_ref[e:e + 1, :]
         place[e] = nt(token_slot(row), row_slot(row, z)).astype(BF16)
@@ -349,14 +330,7 @@
 
     for copy in sends:
         copy.wait_send()
-    for e in range(exp_dev):
-        target = lane_of(e, feat_half, own_b)
-
-        @pl.when(target != lane)
-        def _():
-            send_rows(0, e).wait_send()
-            remote(gathered.at[e], rx.at[feat_pos], m_send.at[e], m_recv.at[feat_pos], z, target).wait_send()
-
+    finish_rows(1)
     for j in range(exp_dev):
         @pl.when(own_h * half_lanes + j * blocks + own_b != lane)
         def _():
@@ -422,14 +396,12 @@
             pltpu.VMEM((capacity, hidden), BF16),
             pltpu.VMEM((capacity, hidden), BF16),
             pltpu.VMEM((tok_dev, width), BF16),
+            pltpu.VMEM((tok_dev, width), BF16),
             pltpu.VMEM((exp_dev, capacity), F32),
             pltpu.VMEM((experts, capacity), jnp.int32),
             pltpu.VMEM((half_width, hidden), BF16),
             pltpu.VMEM((half_width, hidden), BF16),
             pltpu.VMEM((hidden, half_width), BF16),
-            pltpu.VMEM((groups, tok_dev, width), BF16),
-            pltpu.VMEM((exp_dev, capacity, width), BF16),
-            pltpu.VMEM((half_lanes, capacity, width), BF16),
             pltpu.VMEM((capacity, half_width), BF16),
             pltpu.VMEM((3, capacity, hidden), F32),
             pltpu.VMEM((3, chunks, capacity, chunk), BF16),
@@ -437,17 +409,17 @@
             pltpu.VMEM((exp_dev, blocks, 8, capacity), F32),
             pltpu.VMEM((blocks, exp_dev, capacity, width), BF16),
             pltpu.VMEM((blocks, exp_dev, capacity, width), BF16),
-            pltpu.VMEM((groups, exp_dev, peer, width), BF16),
-            pltpu.VMEM((half_lanes, groups, peer, width), BF16),
+            pltpu.VMEM((2, groups, exp_dev, peer, width), BF16),
+            pltpu.VMEM((2, half_lanes, groups, peer, width), BF16),
             pltpu.VMEM((exp_dev, groups, peer, width), BF16),
             pltpu.VMEM((experts, peer, width), BF16),
             pltpu.VMEM((experts, tok_dev, peer), BF16),
-            dma((7,)), dma((groups,)), dma((groups,)),
-            dma((exp_dev,)), dma((half_lanes,)), dma((exp_dev, blocks)),
+            pltpu.VMEM((half_lanes, capacity, width), F32),
+            dma((7,)),
             dma((3, chunks)), dma((3, chunks)),
             dma((lanes,)), dma((exp_dev, blocks)),
             dma((blocks, exp_dev)), dma((blocks, exp_dev)),
-            dma((groups, exp_dev)), dma((half_lanes, groups)), dma((exp_dev, groups, blocks)),
+            dma((2, groups, exp_dev)), dma((2, half_lanes, groups)), dma((2, exp_dev, groups, blocks)),
             dma((exp_dev, groups)), dma((experts,)),
         ],
         compiler_params=pltpu.CompilerParams(

time: 53.3 us -> 48.7 us (0.914)
  Pallas kernels: 52.5 us -> 47.7 us
    pallas_call x1, Pallas kernels: 49.7 us -> 45 us  [local(): pl.pallas_call(functools.partial(layer_kernel, dims), out_shape=results,...]
where the time goes in v1:
time: 48.7 us; the launch traced here: 48.4 us
  Pallas kernels  47.7 us (98%)
  between operations  0.64 us (1%)
    pallas_call x1, Pallas kernels, local(): pl.pallas_call(functools.partial(layer_kernel, dims), out_shape=results,...  45 us
    pallas_call x1, Pallas kernels, local(): pl.pallas_call(write_kernel, out_shape=results, in_specs=[anywhere] * 5,...  2.77 us

profile of v1, /device:TPU:2, one launch (start us, length us, event | category | flops | bytes accessed | tf_op | source)
XLA Modules:
  0.0 48.4 jit_solution(11920764299893460685)
XLA Ops:
  0.6 45.0 %layer.1 = (bf16[128,256]{1,0:T(8,128)(2,1)S(1)}, f32[2,128]{1,0:T(2,128)S(1)}, bf16[1,1024,1024]{2,1,0:T(8,128)(2,1)S(1)}, bf16[1,1024,1024]{2,1,0:T(8,128)(2,1)S(1)}, bf16[1,1024,1024]{2,1,0:T(8,128)(2,1)S(1)}) custom-call(bf16[128,256]{1,0:T(8,128)(2,1)} %x_hbm.1, bf16[128,256]{1,0:T(8,128)(2,1)} %cot_hbm.1, bf16[1,1024,1024]{2,1,0:T(8,128)(2,1)} %wg_hbm.1, ...), custom_call_target="tpu_custom_call" | custom-call | tf_op jit(solution)/shard_map/layer/pallas_call | solution.py:387
  45.6 2.8 %write_out.1 = (bf16[128,256]{1,0:T(8,128)(2,1)}, f32[2,128]{1,0:T(2,128)}, bf16[1,1024,1024]{2,1,0:T(8,128)(2,1)}, bf16[1,1024,1024]{2,1,0:T(8,128)(2,1)}, bf16[1,1024,1024]{2,1,0:T(8,128)(2,1)}) custom-call(bf16[128,256]{1,0:T(8,128)(2,1)S(1)} %get-tuple-element.15.refs_0_, f32[2,128]{1,0:T(2,128)S(1)} %get-tuple-element.16.refs_1_, ...), custom_call_target="tpu_custom_call" | custom-call | tf_op jit(solution)/shard_map/write_out/pallas_call | solution.py:430

commit v2 on v1

--- a/solution.py
+++ b/solution.py
@@ -30,7 +30,7 @@
     tokens_ref, terms_ref, grad_gate, grad_up, grad_down,
     rows_in_ref, scaled_ref, act_ref, dgate_ref, dup_ref,
     x_ref, cot_ref, combine_ref, idx_ref, wg, wu, wd, rows_out, mine, ex_send, ex_recv,
-    term_buf, red_send, red_recv, xs_send, xs_recv, bk_send, bk_recv, place, acc,
+    term_buf, red_send, red_recv, xs_send, xs_recv, bk_send, bk_recv, place, acc, rows_in_t,
     w_sem, x_send, x_recv,
     c_send, c_recv, r_send, r_recv, s_send, s_recv, sf_send, k_send, k_recv,
 ):
@@ -70,7 +70,6 @@
 
     barrier = pltpu.get_barrier_semaphore()
     for d in range(1, groups):
-        pl.semaphore_signal(barrier, inc=1, device_id=(lax.rem(z + d, groups), lane), device_id_type=MESH)
         for e in range(exp_dev):
             for other in (lane_of(e, feat_half, own_b), own_h * half_lanes + e * blocks + own_b):
                 pl.semaphore_signal(barrier, inc=1, device_id=(lax.rem(z + d, groups), other), device_id_type=MESH)
@@ -103,7 +102,7 @@
             xs_send[0, d, e] = nn(pick, x_ref[...]).astype(BF16)
             xs_send[1, d, e] = nn(pick, cot_ref[...]).astype(BF16)
 
-    pl.semaphore_wait(barrier, lanes - 1 + (groups - 1) * (1 + 2 * exp_dev))
+    pl.semaphore_wait(barrier, lanes - 1 + (groups - 1) * 2 * exp_dev)
 
     sends = []
 
@@ -212,6 +211,12 @@
         cols = slice(c * chunk, (c + 1) * chunk)
         exchange_sum(2, c, nt(rows_out[...], wd[cols, :]))
 
+    from_slots = slot_map(0)
+    for e in range(experts):
+        row = idx_ref[e:e + 1, :]
+        place[e] = nt(token_slot(row), row_slot(row, z)).astype(BF16)
+    rows_in_t[...] = rows_in_ref[...].T
+
     def sum_arrived(which, c):
         arrived(ex_recv.at[which, c], x_send.at[which, c], x_recv.at[which, c])
         return mine[which, :, c * chunk:(c + 1) * chunk] + ex_recv[which, c].astype(F32)
@@ -258,8 +263,6 @@
                           z, lane_of(own_e, own_h, to_b))
             copy.start()
             sends.append(copy)
-    from_slots = slot_map(0)
-
     def send_back(j, d):
         g = lax.rem(z + d, groups)
         slot = z * exp_dev + own_e
@@ -299,12 +302,8 @@
     step = min(half_width, 256)
     for i in range(half_width // step):
         cols = slice(i * step, (i + 1) * step)
-        grad_gate[0, cols, :] = tn(rows_in_ref[:, cols], dgate_ref[...]).astype(BF16)
-        grad_up[0, cols, :] = tn(rows_in_ref[:, cols], dup_ref[...]).astype(BF16)
-    for e in range(experts):
-        row = idx_ref[e:e + 1, :]
-        place[e] = nt(token_slot(row), row_slot(row, z)).astype(BF16)
-
+        grad_gate[0, cols, :] = nn(rows_in_t[cols, :], dgate_ref[...]).astype(BF16)
+        grad_up[0, cols, :] = nn(rows_in_t[cols, :], dup_ref[...]).astype(BF16)
     for e in range(exp_dev):
         for b in range(blocks):
             @pl.when(lane_of(e, 0, b) != lane)
@@ -415,6 +414,7 @@
             pltpu.VMEM((experts, peer, width), BF16),
             pltpu.VMEM((experts, tok_dev, peer), BF16),
             pltpu.VMEM((half_lanes, capacity, width), F32),
+            pltpu.VMEM((half_width, capacity), BF16),
             dma((7,)),
             dma((3, chunks)), dma((3, chunks)),
             dma((lanes,)), dma((exp_dev, blocks)),

time: 48.7 us -> 48.7 us (level)
  no operation moved by 1% of the time
where the time goes in v2:
time: 48.7 us; the launch traced here: 48.4 us
  Pallas kernels  47.8 us (98%)
  between operations  0.64 us (1%)
    pallas_call x1, Pallas kernels, local(): pl.pallas_call(functools.partial(layer_kernel, dims), out_shape=results,...  45 us
    pallas_call x1, Pallas kernels, local(): pl.pallas_call(write_kernel, out_shape=results, in_specs=[anywhere] * 5,...  2.77 us

profile of v2, /device:TPU:2, one launch (start us, length us, event | category | flops | bytes accessed | tf_op | source)
XLA Modules:
  0.0 48.4 jit_solution(6426841107943390061)
XLA Ops:
  0.6 45.0 %layer.1 = (bf16[128,256]{1,0:T(8,128)(2,1)S(1)}, f32[2,128]{1,0:T(2,128)S(1)}, bf16[1,1024,1024]{2,1,0:T(8,128)(2,1)S(1)}, bf16[1,1024,1024]{2,1,0:T(8,128)(2,1)S(1)}, bf16[1,1024,1024]{2,1,0:T(8,128)(2,1)S(1)}) custom-call(bf16[128,256]{1,0:T(8,128)(2,1)} %x_hbm.1, bf16[128,256]{1,0:T(8,128)(2,1)} %cot_hbm.1, bf16[1,1024,1024]{2,1,0:T(8,128)(2,1)} %wg_hbm.1, ...), custom_call_target="tpu_custom_call" | custom-call | tf_op jit(solution)/shard_map/layer/pallas_call | solution.py:386
  45.6 2.8 %write_out.1 = (bf16[128,256]{1,0:T(8,128)(2,1)}, f32[2,128]{1,0:T(2,128)}, bf16[1,1024,1024]{2,1,0:T(8,128)(2,1)}, bf16[1,1024,1024]{2,1,0:T(8,128)(2,1)}, bf16[1,1024,1024]{2,1,0:T(8,128)(2,1)}) custom-call(bf16[128,256]{1,0:T(8,128)(2,1)S(1)} %get-tuple-element.15.refs_0_, f32[2,128]{1,0:T(2,128)S(1)} %get-tuple-element.16.refs_1_, ...), custom_call_target="tpu_custom_call" | custom-call | tf_op jit(solution)/shard_map/write_out/pallas_call | solution.py:430

commit v3 on v2

--- a/solution.py
+++ b/solution.py
@@ -30,7 +30,7 @@
     tokens_ref, terms_ref, grad_gate, grad_up, grad_down,
     rows_in_ref, scaled_ref, act_ref, dgate_ref, dup_ref,
     x_ref, cot_ref, combine_ref, idx_ref, wg, wu, wd, rows_out, mine, ex_send, ex_recv,
-    term_buf, red_send, red_recv, xs_send, xs_recv, bk_send, bk_recv, place, acc, rows_in_t,
+    term_buf, red_send, red_recv, xs_send, xs_recv, bk_send, bk_recv, place, acc, rows_in_t, picks,
     w_sem, x_send, x_recv,
     c_send, c_recv, r_send, r_recv, s_send, s_recv, sf_send, k_send, k_recv,
 ):
@@ -93,14 +93,12 @@
 
     loads[0].wait()
     loads[1].wait()
-    loads[3].wait()
     for d in range(groups):
         g = lax.rem(z + d, groups)
         for e in range(exp_dev):
             row = idx_ref[pl.ds(g * exp_dev + e, 1), :]
-            pick = nt(row_slot(row, z), token_slot(row)).astype(BF16)
-            xs_send[0, d, e] = nn(pick, x_ref[...]).astype(BF16)
-            xs_send[1, d, e] = nn(pick, cot_ref[...]).astype(BF16)
+            picks[d, e] = nt(row_slot(row, z), token_slot(row)).astype(BF16)
+            xs_send[0, d, e] = nn(picks[d, e], x_ref[...]).astype(BF16)
 
     pl.semaphore_wait(barrier, lanes - 1 + (groups - 1) * 2 * exp_dev)
 
@@ -135,6 +133,10 @@
                 send_rows(kind, 0, e).wait_send()
 
     start_rows(0)
+    loads[3].wait()
+    for d in range(groups):
+        for e in range(exp_dev):
+            xs_send[1, d, e] = nn(picks[d, e], cot_ref[...]).astype(BF16)
 
     eye = iota((capacity, capacity), 0) == iota((capacity, capacity), 1)
 
@@ -415,6 +417,7 @@
             pltpu.VMEM((experts, tok_dev, peer), BF16),
             pltpu.VMEM((half_lanes, capacity, width), F32),
             pltpu.VMEM((half_width, capacity), BF16),
+            pltpu.VMEM((groups, exp_dev, peer, tok_dev), BF16),
             dma((7,)),
             dma((3, chunks)), dma((3, chunks)),
             dma((lanes,)), dma((exp_dev, blocks)),

time: 48.7 us -> 50.3 us (1.033)
  Pallas kernels: 47.8 us -> 49.4 us
    pallas_call x1, Pallas kernels: 45 us -> 46.7 us  [local(): pl.pallas_call(functools.partial(layer_kernel, dims), out_shape=results,...]
where the time goes in v3:
time: 50.3 us; the launch traced here: 50.1 us
  Pallas kernels  49.4 us (98%)
  between operations  0.64 us (1%)
    pallas_call x1, Pallas kernels, local(): pl.pallas_call(functools.partial(layer_kernel, dims), out_shape=results,...  46.7 us
    pallas_call x1, Pallas kernels, local(): pl.pallas_call(write_kernel, out_shape=results, in_specs=[anywhere] * 5,...  2.77 us

profile of v3, /device:TPU:2, one launch (start us, length us, event | category | flops | bytes accessed | tf_op | source)
XLA Modules:
  0.0 50.1 jit_solution(5552371341046285934)
XLA Ops:
  0.6 46.7 %layer.1 = (bf16[128,256]{1,0:T(8,128)(2,1)S(1)}, f32[2,128]{1,0:T(2,128)S(1)}, bf16[1,1024,1024]{2,1,0:T(8,128)(2,1)S(1)}, bf16[1,1024,1024]{2,1,0:T(8,128)(2,1)S(1)}, bf16[1,1024,1024]{2,1,0:T(8,128)(2,1)S(1)}) custom-call(bf16[128,256]{1,0:T(8,128)(2,1)} %x_hbm.1, bf16[128,256]{1,0:T(8,128)(2,1)} %cot_hbm.1, bf16[1,1024,1024]{2,1,0:T(8,128)(2,1)} %wg_hbm.1, ...), custom_call_target="tpu_custom_call" | custom-call | tf_op jit(solution)/shard_map/layer/pallas_call | solution.py:388
  47.3 2.8 %write_out.1 = (bf16[128,256]{1,0:T(8,128)(2,1)}, f32[2,128]{1,0:T(2,128)}, bf16[1,1024,1024]{2,1,0:T(8,128)(2,1)}, bf16[1,1024,1024]{2,1,0:T(8,128)(2,1)}, bf16[1,1024,1024]{2,1,0:T(8,128)(2,1)}) custom-call(bf16[128,256]{1,0:T(8,128)(2,1)S(1)} %get-tuple-element.15.refs_0_, f32[2,128]{1,0:T(2,128)S(1)} %get-tuple-element.16.refs_1_, ...), custom_call_target="tpu_custom_call" | custom-call | tf_op jit(solution)/shard_map/write_out/pallas_call | solution.py:433
